TPU v7x, 128 devices: a whole 4x4x4 slice. The times are simulated.
128 devices in a mesh: fsdp: 4 (over z), expert: 32 (over x, y, core).
Axes of the slice: x: 4, y: 4, z: 4, core: 2. Of those that a mesh axis runs over, the one named last changes fastest.
Arguments:
- inputs: bfloat16 [4, 2048, 2048], P(None, ('fsdp', 'expert')), may hold values from -6 to 6
- cache_keys: bfloat16 [2048, 128, 256], P(('fsdp', 'expert'))
- cache_values: bfloat16 [2048, 128, 256], P(('fsdp', 'expert')), may hold values from -6 to 6
- lengths: int32 [2048], P(('fsdp', 'expert')), may hold values from 2 to 128, as said below
- new_keys: bfloat16 [4, 2048, 256], P(None, ('fsdp', 'expert')), may hold values from -6 to 6
- new_values: bfloat16 [4, 2048, 256], P(None, ('fsdp', 'expert')), may hold values from -6 to 6
- queries: bfloat16 [4, 2048, 2048], P(None, ('fsdp', 'expert'))
- out_weight: bfloat16 [2048, 2048], P('fsdp'), may hold values from -0.125 to 0.125
- norm_gain: bfloat16 [2048], replicated, may hold values from 0.099609375 to 1.8984375
- router: bfloat16 [2048, 128], replicated
- experts: int32 [4, 2048, 8], P(None, ('fsdp', 'expert')), may hold values from 0 to 127, all different within a row; in each aligned block of 16 rows (0 to 15, 16 to 31, ..., all dimensions but the last counted through in order) at most 2 rows name the same one
- master_gate: float32 [128, 2048, 768], P('fsdp', 'expert'), may hold values from -0.125 to 0.125
- master_up: float32 [128, 2048, 768], P('fsdp', 'expert'), may hold values from -0.125 to 0.125
- master_down: float32 [128, 2048, 768], P('fsdp', 'expert'), may hold values from -0.4375 to 0.4375
Outputs:
- outputs: bfloat16 [4, 2048, 2048], P(None, ('fsdp', 'expert'))
Inputs may be any that keep to these rules, and one draw needn't show every extreme that they name: Each row names 8 different experts. In each step the 16 rows of one device name any one expert at most 2 times, a bound that some block reaches by one device's rows. `lengths`: some row has a full cache.
All inputs are finite; a program needn't handle non-finite values.
Results may differ from a plain program's by a relative error of at most 0.006.
Values may be sent and summed in bfloat16 or wider, within the bound.
A program may use at most 128 MiB of HBM per device.

v0:
```python
import functools
import math

import jax
import jax.numpy as jnp
from jax import lax
from jax.experimental import pallas as pl
from jax.experimental.pallas import tpu as pltpu
from jax.sharding import PartitionSpec as P

MESH = pl.DeviceIdType.MESH
BF = jnp.bfloat16
F32 = jnp.float32
NT = (((1,), (1,)), ((), ()))
TN = (((0,), (0,)), ((), ()))
DEPTH = 8


def dot(a, b):
    return jnp.dot(a, b, preferred_element_type=F32)


def dot_nt(a, b):
    return lax.dot_general(a, b, NT, preferred_element_type=F32)


def dot_tn(a, b):
    return lax.dot_general(a, b, TN, preferred_element_type=F32)


def kernel(
    x_ref, q_ref, ck_ref, cv_ref, nk_ref, nv_ref, len_ref, gain_ref, router_ref, ids_ref,
    wo_ref, mg_ref, mu_ref, md_ref,
    out_ref,
    stage, ws, mid_a, mid_b, wgu, wd, wout, ag_a, ag_b, ssend, srecv,
    o_s, att, resid, pg, rs1, rs2, mix,
    st_sem, w1_s, w1_r, w2_s, w2_r, d2_s, d2_r, own_sem, o_snd, o_rcv, f_snd, f_rcv,
    ag_s, ag_r, z_s, z_r, t_s, t_r, r1_s, r1_r, r2_s, r2_r,
):
    z = lax.axis_index("fsdp")
    e = lax.axis_index("expert")
    x = e // 8
    y = (e // 2) % 4
    c = e % 2
    me = z * 2 + c

    def dev(dx=0, dy=0, dc=0, dz=0):
        return (
            (z + dz) % 4,
            ((x + dx) % 4) * 8 + ((y + dy) % 4) * 2 + (c + dc) % 2,
        )

    def remote(src, dst, snd, rcv, target):
        return pltpu.make_async_remote_copy(
            src_ref=src, dst_ref=dst, send_sem=snd, recv_sem=rcv,
            device_id=target, device_id_type=MESH,
        )

    masters = (mg_ref, mu_ref, md_ref)

    def load(t, j, slot):
        return pltpu.make_async_copy(masters[t].at[j // 4, j % 4], stage.at[slot], st_sem.at[slot])

    for j in range(DEPTH):
        load(0, j, j).start()
    own_out = pltpu.make_async_copy(wo_ref, wout.at[pl.ds(z * 4, 4)], own_sem)
    own_out.start()

    partners = [(d, 0, k, 0) for d in (1, 2, 3) for k in (0, 1)]
    partners += [(0, d, k, 0) for d in (1, 2, 3) for k in (0, 1)]
    partners += [(0, 0, k, d) for d in (1, 2, 3) for k in (0, 1)]
    partners += [(0, 0, 1, 0)]
    barrier = pltpu.get_barrier_semaphore()
    for p in partners:
        pl.semaphore_signal(barrier, inc=1, device_id=dev(*p), device_id_type=MESH)
    pl.semaphore_wait(barrier, len(partners))

    drains = []

    gathers = []
    for dz in (1, 2, 3):
        cp = remote(
            wo_ref.at[pl.ds(c * 2, 2)], wout.at[pl.ds(z * 4 + c * 2, 2)],
            o_snd.at[dz - 1], o_rcv.at[dz - 1], dev(dz=dz),
        )
        cp.start()
        gathers.append(cp)

    first = []
    for t in range(3):
        def cast(j, slot_t):
            slot = j % DEPTH
            load(t, j, slot).wait()
            ws[t, j // 4, j % 4] = stage[slot].astype(BF)
            return slot

        def step_a(j, carry):
            slot = cast(j, t)
            load(t, j + DEPTH, slot).start()
            return carry

        def step_b(j, carry):
            slot = cast(j, t)
            if t < 2:
                load(t + 1, j - DEPTH, slot).start()
            return carry

        lax.fori_loop(0, 16 - DEPTH, step_a, 0)
        lax.fori_loop(16 - DEPTH, 16, step_b, 0)
        group = []
        for d in (1, 3, 2, 0):
            for dc in (0, 1):
                i = d * 2 + dc
                xd, yd, cd = (x + d) % 4, (y + d) % 4, (c + dc) % 2
                src_a = ws.at[t, xd, :, cd, :, pl.ds(0, 384)]
                src_b = ws.at[t, :, yd, cd, :, pl.ds(384, 384)]
                if i == 0:
                    cp_a = pltpu.make_async_copy(src_a, mid_a.at[t, x, c], w1_r.at[t, 0, i])
                    cp_b = pltpu.make_async_copy(src_b, mid_b.at[t, y, c], w1_r.at[t, 1, i])
                else:
                    cp_a = remote(
                        src_a, mid_a.at[t, x, c], w1_s.at[t, 0, i], w1_r.at[t, 0, i],
                        dev(dx=d, dc=dc),
                    )
                    cp_b = remote(
                        src_b, mid_b.at[t, y, c], w1_s.at[t, 1, i], w1_r.at[t, 1, i],
                        dev(dy=d, dc=dc),
                    )
                    drains += [cp_a, cp_b]
                cp_a.start()
                cp_b.start()
                group += [(i, cp_a), (i, cp_b)]
        first.append(group)

    def wait_group(group):
        for i, cp in group:
            if i == 0:
                cp.wait()
            else:
                cp.wait_recv()

    def second(t, k):
        group = []
        for d in (1, 3, 2, 0):
            xd, yd = (x + d) % 4, (y + d) % 4
            if k is None:
                src_a, src_b = mid_a.at[t, :, :, yd], mid_b.at[t, :, :, xd]
                dst_a = wgu.at[t, :, y, :, :, pl.ds(0, 384)]
                dst_b = wgu.at[t, x, :, :, :, pl.ds(384, 384)]
                snd, rcv = w2_s.at[t], w2_r.at[t]
            else:
                src_a = mid_a.at[t, :, :, yd, pl.ds(16 * k, 16)]
                src_b = mid_b.at[t, :, :, xd, pl.ds(16 * k, 16)]
                dst_a = wd.at[k, :, y, :, :, pl.ds(0, 384)]
                dst_b = wd.at[k, x, :, :, :, pl.ds(384, 384)]
                snd, rcv = d2_s.at[k], d2_r.at[k]
            if d == 0:
                cp_a = pltpu.make_async_copy(src_a, dst_a, rcv.at[0, 0])
                cp_b = pltpu.make_async_copy(src_b, dst_b, rcv.at[1, 0])
            else:
                cp_a = remote(src_a, dst_a, snd.at[0, d], rcv.at[0, d], dev(dy=d))
                cp_b = remote(src_b, dst_b, snd.at[1, d], rcv.at[1, d], dev(dx=d))
                drains.extend([cp_a, cp_b])
            cp_a.start()
            cp_b.start()
            group += [(d, cp_a), (d, cp_b)]
        return group

    inv = 1.0 / math.sqrt(128.0)
    neg = -jnp.inf
    lane = lax.broadcasted_iota(jnp.int32, (32, 128), 1)
    fresh_ok = lax.broadcasted_iota(jnp.int32, (32, 16), 1) <= (
        lax.broadcasted_iota(jnp.int32, (32, 16), 0) >> 3
    )

    def attend(r, carry):
        ok = lane < len_ref[r]
        for g in range(2):
            cols = slice(g * 128, (g + 1) * 128)
            qq = q_ref[r, g]
            s = jnp.where(ok, dot_nt(qq, ck_ref[r, :, cols]) * inv, neg)
            f = jnp.where(fresh_ok, dot_nt(qq, nk_ref[r, :, cols]) * inv, neg)
            top = jnp.maximum(
                jnp.max(s, axis=-1, keepdims=True), jnp.max(f, axis=-1, keepdims=True)
            )
            es, ef = jnp.exp(s - top), jnp.exp(f - top)
            total = jnp.sum(es, axis=-1, keepdims=True) + jnp.sum(ef, axis=-1, keepdims=True)
            ps, pf = (es / total).astype(BF), (ef / total).astype(BF)
            o_s[r, g] = dot(ps, cv_ref[r, :, cols]) + dot(pf, nv_ref[r, :, cols])
        return carry

    lax.fori_loop(0, 16, attend, 0)
    for g in range(2):
        for h in range(8):
            for t in range(4):
                head = g * 8 + h
                att[t * 16:(t + 1) * 16, head * 128:(head + 1) * 128] = o_s[
                    :, g, t * 8 + h, :
                ].astype(BF)

    forwards = []
    for dz in (1, 2, 3):
        gathers[dz - 1].wait_recv()
        part = wout.at[pl.ds(((z + 4 - dz) % 4) * 4 + c * 2, 2)]
        cp = remote(part, part, f_snd.at[dz - 1], f_rcv.at[dz - 1], dev(dc=1))
        cp.start()
        forwards.append(cp)
    wait_group(first[0])
    g2 = second(0, None)
    own_out.wait()
    for cp in gathers:
        cp.wait_send()
    for cp in forwards:
        cp.wait()

    def project(n, carry):
        cols = pl.ds(pl.multiple_of(n * 512, 512), 512)
        w = wout[:, :, :, cols].reshape(2048, 512)
        resid[:, cols] = x_ref[:, cols].astype(F32) + dot(att[...], w)
        return carry

    lax.fori_loop(0, 4, project, 0)
    res = resid[...]
    mean_square = jnp.mean(res * res, axis=-1, keepdims=True)
    normed = (res * lax.rsqrt(mean_square + 1e-06) * gain_ref[...].astype(F32)).astype(BF)
    ag_a[y, x, :, 0:1024] = normed[:, 0:1024]
    ag_b[x, y] = normed[:, 1024:2048]
    logits = dot(normed, router_ref[...])
    column = lax.broadcasted_iota(jnp.int32, (64, 128), 1)
    member = jnp.zeros((64, 128), F32)
    for k in range(8):
        member = member + (ids_ref[:, k:k + 1] == column).astype(F32)
    row_i = lax.broadcasted_iota(jnp.int32, (64, 64), 0)
    col_i = lax.broadcasted_iota(jnp.int32, (64, 64), 1)
    before = ((row_i >> 4) == (col_i >> 4)) & (col_i < row_i)
    rank = dot(before.astype(F32).astype(BF), member.astype(BF))
    chosen = jnp.where(member > 0.5, logits, neg)
    chosen_exp = jnp.exp(chosen - jnp.max(chosen, axis=-1, keepdims=True))
    gates = chosen_exp / jnp.sum(chosen_exp, axis=-1, keepdims=True)
    ag_a[y, x, :, 1024:1152] = jnp.where(rank < 0.5, gates, -gates).astype(BF)

    ag1 = []
    for d in (1, 3, 2):
        cp_a = remote(
            ag_a.at[y, x], ag_a.at[y, x], ag_s.at[0, d], ag_r.at[0, d], dev(dx=d)
        )
        cp_b = remote(
            ag_b.at[x, y], ag_b.at[x, y], ag_s.at[1, d], ag_r.at[1, d], dev(dy=d)
        )
        cp_a.start()
        cp_b.start()
        ag1 += [cp_a, cp_b]
    wait_group(first[1])
    u2 = second(1, None)
    for cp in ag1:
        cp.wait()
    ag2 = []
    for d in (1, 3, 2):
        cp_a = remote(ag_a.at[y], ag_a.at[y], ag_s.at[2, d], ag_r.at[2, d], dev(dy=d))
        cp_b = remote(ag_b.at[x], ag_b.at[x], ag_s.at[3, d], ag_r.at[3, d], dev(dx=d))
        cp_a.start()
        cp_b.start()
        ag2 += [cp_a, cp_b]
    wait_group(first[2])
    d2 = [second(2, k) for k in range(4)]
    for cp in ag2:
        cp.wait()

    e_row = lax.broadcasted_iota(jnp.int32, (8, 128), 0)
    e_lane = lax.broadcasted_iota(jnp.int32, (8, 128), 1)
    pick = (e_lane == (e_row >> 1) * 32 + (e_row & 1) + x * 8 + y * 2).astype(F32).astype(BF)
    slot_i = lax.broadcasted_iota(jnp.int32, (8, 32, 256), 1)
    row_of = lax.broadcasted_iota(jnp.int32, (8, 32, 256), 2)
    same = (row_of >> 4) == (slot_i >> 1)
    sign = jnp.where((slot_i & 1) == 0, 1.0, -1.0).astype(F32)

    def select(t, carry):
        rows = pl.ds(pl.multiple_of(t * 16, 16), 16)
        dst = pl.ds(pl.multiple_of((t % 2) * 32, 32), 32)
        aux = ag_a[:, :, rows, 1024:1152].reshape(256, 128)
        code = dot_nt(pick, aux)
        signed = jnp.where(same, code[:, None, :] * sign, 0.0)
        weight = jnp.maximum(signed, 0.0).reshape(256, 256)
        pg[t] = weight.astype(BF)
        place = (weight > 0.0).astype(F32).astype(BF)
        for n in range(2):
            cols = slice(n * 512, (n + 1) * 512)
            got = dot(place, ag_a[:, :, rows, cols].reshape(256, 512))
            ssend[:, t // 2, dst, cols] = got.astype(BF).reshape(8, 32, 512)
        for n in range(2):
            cols = slice(n * 512, (n + 1) * 512)
            part = jnp.concatenate(
                [ag_b[:, k, rows, cols].reshape(64, 512) for k in range(4)], axis=0
            )
            got = dot(place, part)
            ssend[:, t // 2, dst, n * 512 + 1024:n * 512 + 1536] = got.astype(BF).reshape(8, 32, 512)
        return carry

    lax.fori_loop(0, 4, select, 0)

    column_devs = [(dz, dc) for dz in (1, 3, 2, 0) for dc in (0, 1)]
    dispatch = []
    for dz, dc in column_devs:
        i = dz * 2 + dc
        to = ((z + dz) % 4) * 2 + (c + dc) % 2
        if i == 0:
            cp = pltpu.make_async_copy(ssend.at[me], srecv.at[me], z_r.at[i])
        else:
            cp = remote(ssend.at[to], srecv.at[me], z_s.at[i], z_r.at[i], dev(dz=dz, dc=dc))
        cp.start()
        dispatch.append(cp)
    wait_group(g2)
    wait_group(u2)
    for cp in dispatch:
        cp.wait()

    def hide(i, carry):
        rows = srecv[pl.ds(i * 2, 2)].reshape(256, 2048)
        gate = dot(rows, wgu[0].reshape(2048, 768))
        up = dot(rows, wgu[1].reshape(2048, 768))
        ag_b[i, :, :, 0:768] = (jax.nn.silu(gate) * up).astype(BF).reshape(4, 64, 768)
        return carry

    lax.fori_loop(0, 4, hide, 0)

    def down(k):
        cols = slice(k * 512, (k + 1) * 512)
        wait_group(d2[k])

        def tile(i, carry):
            hidden = ag_b[i, :, :, 0:768].reshape(256, 768)
            got = dot_nt(hidden, wd[k].reshape(512, 768))
            srecv[pl.ds(i * 2, 2), :, :, cols] = got.astype(BF).reshape(2, 2, 64, 512)
            return carry

        lax.fori_loop(0, 4, tile, 0)
        group = []
        for dz, dc in column_devs:
            i = dz * 2 + dc
            to = ((z + dz) % 4) * 2 + (c + dc) % 2
            dst = wout.at[me, :, :, pl.ds(k * 512, 512)]
            if i == 0:
                cp = pltpu.make_async_copy(
                    srecv.at[me, :, :, pl.ds(k * 512, 512)], dst, t_r.at[k, i]
                )
            else:
                cp = remote(
                    srecv.at[to, :, :, pl.ds(k * 512, 512)], dst, t_s.at[k, i], t_r.at[k, i],
                    dev(dz=dz, dc=dc),
                )
                drains.append(cp)
            cp.start()
            group.append((i, cp))
        return group

    def combine(k, group):
        wait_group(group)

        def tile(t, carry):
            rows = pl.ds(pl.multiple_of(t * 16, 16), 16)
            src = pl.ds(pl.multiple_of((t % 2) * 32, 32), 32)
            got = wout[0:8, t // 2, src, k * 512:(k + 1) * 512].reshape(256, 512)
            part = dot_tn(pg[t], got).astype(BF)
            wout[8:16, :, rows, k * 512:k * 512 + 256] = part[:, 0:256].reshape(8, 2, 16, 256)
            for yy in range(4):
                for xx in range(4):
                    b = (yy * 4 + xx) * 16
                    wout[8 + xx * 2 + yy // 2, yy % 2, rows, k * 512 + 256:(k + 1) * 512] = part[
                        b:b + 16, 256:512
                    ]
            return carry

        lax.fori_loop(0, 4, tile, 0)
        sums = []
        for d in (1, 3, 2):
            xd, yd = (x + d) % 4, (y + d) % 4
            cp_a = remote(
                wout.at[pl.ds(8 + yd * 2, 2), :, :, pl.ds(k * 512, 256)], rs1.at[k, 0, d - 1],
                r1_s.at[k, 0, d - 1], r1_r.at[k, 0, d - 1], dev(dy=d),
            )
            cp_b = remote(
                wout.at[pl.ds(8 + xd * 2, 2), :, :, pl.ds(k * 512 + 256, 256)],
                rs1.at[k, 1, d - 1],
                r1_s.at[k, 1, d - 1], r1_r.at[k, 1, d - 1], dev(dx=d),
            )
            cp_a.start()
            cp_b.start()
            sums += [cp_a, cp_b]
        drains.extend(sums)
        return sums

    def halfway(k, sums):
        for cp in sums:
            cp.wait_recv()
        for route in range(2):
            mine = (y, x)[route]
            lanes = slice(k * 512 + route * 256, k * 512 + route * 256 + 256)
            total = wout[pl.ds(8 + mine * 2, 2), :, :, lanes].reshape(256, 256).astype(F32)
            for d in range(3):
                total = total + rs1[k, route, d].reshape(256, 256).astype(F32)
            ag_a[k, :, :, route * 256:(route + 1) * 256] = total.astype(BF).reshape(4, 64, 256)
        group = []
        for d in (1, 3, 2):
            xd, yd = (x + d) % 4, (y + d) % 4
            cp_a = remote(
                ag_a.at[k, xd, :, pl.ds(0, 256)], rs2.at[k, 0, d - 1],
                r2_s.at[k, 0, d - 1], r2_r.at[k, 0, d - 1], dev(dx=d),
            )
            cp_b = remote(
                ag_a.at[k, yd, :, pl.ds(256, 256)], rs2.at[k, 1, d - 1],
                r2_s.at[k, 1, d - 1], r2_r.at[k, 1, d - 1], dev(dy=d),
            )
            cp_a.start()
            cp_b.start()
            group += [cp_a, cp_b]
        drains.extend(group)
        return group

    def close(k, group):
        for cp in group:
            cp.wait_recv()
        for route in range(2):
            mine = (x, y)[route]
            total = ag_a[k, mine, :, route * 256:(route + 1) * 256].astype(F32)
            for d in range(3):
                total = total + rs2[k, route, d].astype(F32)
            mix[:, k * 512 + route * 256:k * 512 + (route + 1) * 256] = total

    backs, sums, ends = {}, {}, {}
    for k in range(7):
        if k < 4:
            backs[k] = down(k)
        if 0 <= k - 1 < 4:
            sums[k - 1] = combine(k - 1, backs[k - 1])
        if 0 <= k - 2 < 4:
            ends[k - 2] = halfway(k - 2, sums[k - 2])
        if 0 <= k - 3 < 4:
            close(k - 3, ends[k - 3])

    p_i = lax.broadcasted_iota(jnp.int32, (512, 512), 0)
    o_i = lax.broadcasted_iota(jnp.int32, (512, 512), 1)
    perm = (o_i == ((p_i >> 4) & 7) * 64 + (p_i >> 7) * 16 + (p_i & 15)).astype(F32).astype(BF)
    for g in range(4):
        v = jnp.concatenate(
            [mix[:, k * 512 + g * 128:k * 512 + (g + 1) * 128] for k in range(4)], axis=1
        )
        hi = v.astype(BF)
        lo = (v - hi.astype(F32)).astype(BF)
        out_ref[:, g * 512:(g + 1) * 512] = (
            resid[:, g * 512:(g + 1) * 512] + dot(hi, perm) + dot(lo, perm)
        )
    for cp in drains:
        cp.wait_send()


def per_device(
    inputs, cache_keys, cache_values, lengths, new_keys, new_values, queries, out_weight,
    norm_gain, router, experts, master_gate, master_up, master_down,
):
    q = queries.reshape(4, 16, 2, 8, 128).transpose(1, 2, 0, 3, 4).reshape(16, 2, 32, 128)
    nk = jnp.pad(new_keys.transpose(1, 0, 2), ((0, 0), (0, 12), (0, 0)))
    nv = jnp.pad(new_values.transpose(1, 0, 2), ((0, 0), (0, 12), (0, 0)))
    lens = jnp.broadcast_to(lengths[:, None, None], (16, 1, 128))
    vm = pl.BlockSpec(memory_space=pltpu.VMEM)
    anyspace = pl.BlockSpec(memory_space=pl.ANY)
    dma = pltpu.SemaphoreType.DMA
    shape5 = (4, 4, 2, 64, 768)
    out = pl.pallas_call(
        kernel,
        out_shape=jax.ShapeDtypeStruct((64, 2048), F32),
        in_specs=[vm] * 10 + [anyspace] * 4,
        out_specs=vm,
        scratch_shapes=[
            pltpu.VMEM((DEPTH, 2, 64, 768), F32),
            pltpu.VMEM((3, 4, 4, 2, 64, 768), BF),
            pltpu.VMEM((3, 4, 2, 4, 64, 384), BF),
            pltpu.VMEM((3, 4, 2, 4, 64, 384), BF),
            pltpu.VMEM((2, 4, 4, 2, 64, 768), BF),
            pltpu.VMEM((4, 4, 4, 2, 16, 768), BF),
            pltpu.VMEM((16, 2, 64, 2048), BF),
            pltpu.VMEM((4, 4, 64, 1152), BF),
            pltpu.VMEM((4, 4, 64, 1024), BF),
            pltpu.VMEM((8, 2, 64, 2048), BF),
            pltpu.VMEM((8, 2, 64, 2048), BF),
            pltpu.VMEM((16, 2, 32, 128), F32),
            pltpu.VMEM((64, 2048), BF),
            pltpu.VMEM((64, 2048), F32),
            pltpu.VMEM((4, 256, 256), BF),
            pltpu.VMEM((4, 2, 3, 2, 2, 64, 256), BF),
            pltpu.VMEM((4, 2, 3, 64, 256), BF),
            pltpu.VMEM((64, 2048), F32),
            dma((DEPTH,)),
            dma((3, 2, 8)), dma((3, 2, 8)),
            dma((2, 2, 4)), dma((2, 2, 4)),
            dma((4, 2, 4)), dma((4, 2, 4)),
            dma, dma((3,)), dma((3,)), dma((3,)), dma((3,)),
            dma((4, 4)), dma((4, 4)),
            dma((8,)), dma((8,)),
            dma((4, 8)), dma((4, 8)),
            dma((4, 2, 3)), dma((4, 2, 3)),
            dma((4, 2, 3)), dma((4, 2, 3)),
        ],
        compiler_params=pltpu.CompilerParams(
            collective_id=0, has_side_effects=True, vmem_limit_bytes=65_900_000
        ),
        name="moe_decode",
    )(
        inputs.reshape(64, 2048), q, cache_keys, cache_values, nk, nv, lens,
        norm_gain.reshape(1, 2048), router, experts.reshape(64, 8),
        out_weight.reshape(4, 2, 64, 2048),
        master_gate.reshape(shape5), master_up.reshape(shape5), master_down.reshape(shape5),
    )
    return out.astype(BF).reshape(4, 16, 2048)


def solution(mesh):
    return jax.shard_map(
        per_device,
        mesh=mesh,
        in_specs=(
            P(None, ("fsdp", "expert"), None),
            P(("fsdp", "expert"), None, None),
            P(("fsdp", "expert"), None, None),
            P(("fsdp", "expert")),
            P(None, ("fsdp", "expert"), None),
            P(None, ("fsdp", "expert"), None),
            P(None, ("fsdp", "expert"), None),
            P("fsdp", None),
            P(),
            P(),
            P(None, ("fsdp", "expert"), None),
            P("fsdp", "expert", None),
            P("fsdp", "expert", None),
            P("fsdp", "expert", None),
        ),
        out_specs=P(None, ("fsdp", "expert"), None),
        check_vma=False,
    )
```

profile of v0, /device:TPU:0, one launch (start us, length us, event | category | flops | bytes accessed | tf_op | source)
XLA Modules:
  0.0 263.6 jit_solution(10640610443075308579)
XLA Ops:
  0.0 1.3 broadcast_in_dim.2.len_ref
  1.3 1.3 reshape.36.gain_ref
  2.6 0.8 copy.25
  3.4 0.8 copy.24
  4.2 1.4 copy.18
  5.6 0.7 pad.8.nv_ref
  6.2 0.7 pad.7.nk_ref
  6.9 1.0 copy.19
  7.9 0.8 copy.23
  8.7 253.2 %moe_decode.1 = f32[64,2048]{1,0:T(8,128)} custom-call(bf16[64,2048]{1,0:T(8,128)(2,1)} %bitcast.28, bf16[16,2,32,128]{3,2,1,0:T(8,128)(2,1)} %bitcast.26, bf16[16,128,256]{2,1,0:T(8,128)(2,1)} %ck_ref.1, bf16[16,128,256]{2,1,0:T(8,128)(2,1)} %cv_ref.1, bf16[16,16,256]{2,1,0:T(8,128)(2,1)} %pad.7.nk_ref, bf16[16,16,256]{2,1,0:T(8,128)(2,1)} %pad.8.nv_ref, ...), custom_call_target="tpu_custom_call" | custom-call | tf_op jit(solution)/shard_map/moe_decode/pallas_call | solution.py:468
  261.8 1.8 convert_element_type.6
where the time goes:
time: 264 us
  Pallas kernels  253 us (96%)
  local copies, waits for them, and re-layouts  8.64 us (3%)
    pallas_call x1, Pallas kernels, per_device(): pl.pallas_call(kernel, out_shape=jax.ShapeDtypeStruct((64, 2048), F32), i...  253 us

commit v1 on v0

--- a/solution.py
+++ b/solution.py
@@ -14,6 +14,7 @@
 NT = (((1,), (1,)), ((), ()))
 TN = (((0,), (0,)), ((), ()))
 DEPTH = 8
+UNROLL = 4
 
 
 def dot(a, b):
@@ -29,12 +30,12 @@
 
 
 def kernel(
-    x_ref, q_ref, ck_ref, cv_ref, nk_ref, nv_ref, len_ref, gain_ref, router_ref, ids_ref,
+    x_ref, q_ref, ck_ref, cv_ref, nk_ref, nv_ref, gain_ref, router_ref, ids_ref, len_ref,
     wo_ref, mg_ref, mu_ref, md_ref,
     out_ref,
     stage, ws, mid_a, mid_b, wgu, wd, wout, ag_a, ag_b, ssend, srecv,
-    o_s, att, resid, pg, rs1, rs2, mix,
-    st_sem, w1_s, w1_r, w2_s, w2_r, d2_s, d2_r, own_sem, o_snd, o_rcv, f_snd, f_rcv,
+    o_s, nk_s, nv_s, att, attr, resid, pg, rs1, rs2,
+    st_sem, w1_s, w1_r, w2_s, w2_r, d2_s, d2_r, own_sem, o_snd, o_rcv, f_snd, f_rcv, one_sem,
     ag_s, ag_r, z_s, z_r, t_s, t_r, r1_s, r1_r, r2_s, r2_r,
 ):
     z = lax.axis_index("fsdp")
@@ -63,7 +64,7 @@
 
     for j in range(DEPTH):
         load(0, j, j).start()
-    own_out = pltpu.make_async_copy(wo_ref, wout.at[pl.ds(z * 4, 4)], own_sem)
+    own_out = pltpu.make_async_copy(wo_ref, wout.at[pl.ds(0, 4)], own_sem)
     own_out.start()
 
     partners = [(d, 0, k, 0) for d in (1, 2, 3) for k in (0, 1)]
@@ -77,36 +78,27 @@
 
     drains = []
 
-    gathers = []
-    for dz in (1, 2, 3):
-        cp = remote(
-            wo_ref.at[pl.ds(c * 2, 2)], wout.at[pl.ds(z * 4 + c * 2, 2)],
-            o_snd.at[dz - 1], o_rcv.at[dz - 1], dev(dz=dz),
-        )
-        cp.start()
-        gathers.append(cp)
-
-    first = []
-    for t in range(3):
-        def cast(j, slot_t):
+    def cast(t):
+        def one(j):
             slot = j % DEPTH
             load(t, j, slot).wait()
             ws[t, j // 4, j % 4] = stage[slot].astype(BF)
             return slot
 
         def step_a(j, carry):
-            slot = cast(j, t)
-            load(t, j + DEPTH, slot).start()
+            load(t, j + DEPTH, one(j)).start()
             return carry
 
         def step_b(j, carry):
-            slot = cast(j, t)
+            slot = one(j)
             if t < 2:
-                load(t + 1, j - DEPTH, slot).start()
+                load(t + 1, j + DEPTH - 16, slot).start()
             return carry
 
         lax.fori_loop(0, 16 - DEPTH, step_a, 0)
         lax.fori_loop(16 - DEPTH, 16, step_b, 0)
+
+    def leg_one(t):
         group = []
         for d in (1, 3, 2, 0):
             for dc in (0, 1):
@@ -126,11 +118,11 @@
                         src_b, mid_b.at[t, y, c], w1_s.at[t, 1, i], w1_r.at[t, 1, i],
                         dev(dy=d, dc=dc),
                     )
-                    drains += [cp_a, cp_b]
+                    drains.extend([cp_a, cp_b])
                 cp_a.start()
                 cp_b.start()
                 group += [(i, cp_a), (i, cp_b)]
-        first.append(group)
+        return group
 
     def wait_group(group):
         for i, cp in group:
@@ -166,30 +158,52 @@
             group += [(d, cp_a), (d, cp_b)]
         return group
 
+    cast(0)
+    first = [leg_one(0)]
+    cast(1)
+    first.append(leg_one(1))
+
     inv = 1.0 / math.sqrt(128.0)
     neg = -jnp.inf
     lane = lax.broadcasted_iota(jnp.int32, (32, 128), 1)
-    fresh_ok = lax.broadcasted_iota(jnp.int32, (32, 16), 1) <= (
-        lax.broadcasted_iota(jnp.int32, (32, 16), 0) >> 3
+    for g in range(2):
+        for h in range(8):
+            for t in range(4):
+                head = g * 8 + h
+                o_s[:, g, t * 8 + h, :] = q_ref[t, :, head * 128:(head + 1) * 128].astype(F32)
+    for s in range(8):
+        if s < 4:
+            nk_s[:, s, :] = nk_ref[s].astype(F32)
+            nv_s[:, s, :] = nv_ref[s].astype(F32)
+        else:
+            nk_s[:, s, :] = jnp.zeros((16, 256), F32)
+            nv_s[:, s, :] = jnp.zeros((16, 256), F32)
+    fresh_ok = lax.broadcasted_iota(jnp.int32, (32, 8), 1) <= (
+        lax.broadcasted_iota(jnp.int32, (32, 8), 0) >> 3
     )
 
     def attend(r, carry):
         ok = lane < len_ref[r]
         for g in range(2):
             cols = slice(g * 128, (g + 1) * 128)
-            qq = q_ref[r, g]
+            qq = o_s[r, g].astype(BF)
             s = jnp.where(ok, dot_nt(qq, ck_ref[r, :, cols]) * inv, neg)
-            f = jnp.where(fresh_ok, dot_nt(qq, nk_ref[r, :, cols]) * inv, neg)
+            f = jnp.where(fresh_ok, dot_nt(qq, nk_s[r, :, cols].astype(BF)) * inv, neg)
             top = jnp.maximum(
                 jnp.max(s, axis=-1, keepdims=True), jnp.max(f, axis=-1, keepdims=True)
             )
             es, ef = jnp.exp(s - top), jnp.exp(f - top)
             total = jnp.sum(es, axis=-1, keepdims=True) + jnp.sum(ef, axis=-1, keepdims=True)
             ps, pf = (es / total).astype(BF), (ef / total).astype(BF)
-            o_s[r, g] = dot(ps, cv_ref[r, :, cols]) + dot(pf, nv_ref[r, :, cols])
+            o_s[r, g] = dot(ps, cv_ref[r, :, cols]) + dot(pf, nv_s[r, :, cols].astype(BF))
         return carry
 
-    lax.fori_loop(0, 16, attend, 0)
+    def attend_some(i, carry):
+        for j in range(UNROLL):
+            attend(i * UNROLL + j, 0)
+        return carry
+
+    lax.fori_loop(0, 16 // UNROLL, attend_some, 0)
     for g in range(2):
         for h in range(8):
             for t in range(4):
@@ -198,38 +212,70 @@
                     :, g, t * 8 + h, :
                 ].astype(BF)
 
-    forwards = []
-    for dz in (1, 2, 3):
-        gathers[dz - 1].wait_recv()
-        part = wout.at[pl.ds(((z + 4 - dz) % 4) * 4 + c * 2, 2)]
-        cp = remote(part, part, f_snd.at[dz - 1], f_rcv.at[dz - 1], dev(dc=1))
+    toward = []
+    for dz in (1, 3, 2):
+        to = (z + dz) % 4
+        cols = pl.ds(pl.multiple_of(to * 512, 512), 512)
+        cp = remote(att.at[:, cols], attr.at[z], o_snd.at[dz - 1], o_rcv.at[dz - 1], dev(dz=dz))
         cp.start()
-        forwards.append(cp)
-    wait_group(first[0])
-    g2 = second(0, None)
+        toward.append(cp)
+    mine = pltpu.make_async_copy(
+        att.at[:, pl.ds(pl.multiple_of(z * 512, 512), 512)], attr.at[z], one_sem
+    )
+    mine.start()
+    mine.wait()
     own_out.wait()
-    for cp in gathers:
-        cp.wait_send()
-    for cp in forwards:
+    for cp in toward:
         cp.wait()
 
     def project(n, carry):
         cols = pl.ds(pl.multiple_of(n * 512, 512), 512)
-        w = wout[:, :, :, cols].reshape(2048, 512)
-        resid[:, cols] = x_ref[:, cols].astype(F32) + dot(att[...], w)
+        got = dot(attr[...].reshape(256, 512), wout[0:4, :, :, cols].reshape(512, 512))
+        ssend[0:4, 0, :, cols] = got.astype(BF).reshape(4, 64, 512)
         return carry
 
     lax.fori_loop(0, 4, project, 0)
+    partial = []
+    for dz in (1, 3, 2):
+        cp = remote(
+            ssend.at[(z + dz) % 4, 0], rs2.at[dz - 1], f_snd.at[dz - 1], f_rcv.at[dz - 1],
+            dev(dz=dz),
+        )
+        cp.start()
+        partial.append(cp)
+
+    def project_own(n, carry):
+        cols = pl.ds(pl.multiple_of(n * 512, 512), 512)
+        got = dot(attr[z], wout[0:4, :, :, cols].reshape(512, 512))
+        resid[:, cols] = x_ref[:, cols].astype(F32) + got
+        return carry
+
+    lax.fori_loop(0, 4, project_own, 0)
+    cast(2)
+    for cp in partial:
+        cp.wait()
+    for n in range(4):
+        cols = slice(n * 512, (n + 1) * 512)
+        total = resid[:, cols]
+        for d in range(3):
+            total = total + rs2[d, :, cols].astype(F32)
+        resid[:, cols] = total
     res = resid[...]
     mean_square = jnp.mean(res * res, axis=-1, keepdims=True)
-    normed = (res * lax.rsqrt(mean_square + 1e-06) * gain_ref[...].astype(F32)).astype(BF)
+    normed = (res * lax.rsqrt(mean_square + 1e-06) * gain_ref[...].astype(F32).reshape(1, 2048)).astype(BF)
     ag_a[y, x, :, 0:1024] = normed[:, 0:1024]
     ag_b[x, y] = normed[:, 1024:2048]
     logits = dot(normed, router_ref[...])
-    column = lax.broadcasted_iota(jnp.int32, (64, 128), 1)
+    expert_i = lax.broadcasted_iota(jnp.int32, (128, 16), 0)
+    eye_r = lax.broadcasted_iota(jnp.int32, (64, 16), 0)
+    eye_c = lax.broadcasted_iota(jnp.int32, (64, 16), 1)
     member = jnp.zeros((64, 128), F32)
-    for k in range(8):
-        member = member + (ids_ref[:, k:k + 1] == column).astype(F32)
+    for t in range(4):
+        named = jnp.zeros((128, 16), F32)
+        for k in range(8):
+            named = named + (ids_ref[t, k:k + 1, :] == expert_i).astype(F32)
+        eye = (eye_r == eye_c + t * 16).astype(F32).astype(BF)
+        member = member + dot_nt(eye, named.astype(BF))
     row_i = lax.broadcasted_iota(jnp.int32, (64, 64), 0)
     col_i = lax.broadcasted_iota(jnp.int32, (64, 64), 1)
     before = ((row_i >> 4) == (col_i >> 4)) & (col_i < row_i)
@@ -240,31 +286,31 @@
     ag_a[y, x, :, 1024:1152] = jnp.where(rank < 0.5, gates, -gates).astype(BF)
 
     ag1 = []
-    for d in (1, 3, 2):
-        cp_a = remote(
-            ag_a.at[y, x], ag_a.at[y, x], ag_s.at[0, d], ag_r.at[0, d], dev(dx=d)
-        )
-        cp_b = remote(
-            ag_b.at[x, y], ag_b.at[x, y], ag_s.at[1, d], ag_r.at[1, d], dev(dy=d)
-        )
-        cp_a.start()
-        cp_b.start()
-        ag1 += [cp_a, cp_b]
-    wait_group(first[1])
-    u2 = second(1, None)
-    for cp in ag1:
-        cp.wait()
+    for t in range(4):
+        rows = pl.ds(t * 16, 16)
+        group = []
+        for d in (1, 3, 2):
+            part_a, part_b = ag_a.at[y, x, rows], ag_b.at[x, y, rows]
+            cp_a = remote(part_a, part_a, ag_s.at[t, 0, d], ag_r.at[t, 0, d], dev(dx=d))
+            cp_b = remote(part_b, part_b, ag_s.at[t, 1, d], ag_r.at[t, 1, d], dev(dy=d))
+            cp_a.start()
+            cp_b.start()
+            group += [cp_a, cp_b]
+        ag1.append(group)
     ag2 = []
-    for d in (1, 3, 2):
-        cp_a = remote(ag_a.at[y], ag_a.at[y], ag_s.at[2, d], ag_r.at[2, d], dev(dy=d))
-        cp_b = remote(ag_b.at[x], ag_b.at[x], ag_s.at[3, d], ag_r.at[3, d], dev(dx=d))
-        cp_a.start()
-        cp_b.start()
-        ag2 += [cp_a, cp_b]
-    wait_group(first[2])
-    d2 = [second(2, k) for k in range(4)]
-    for cp in ag2:
-        cp.wait()
+    for t in range(4):
+        rows = pl.ds(t * 16, 16)
+        for cp in ag1[t]:
+            cp.wait()
+        group = []
+        for d in (1, 3, 2):
+            part_a, part_b = ag_a.at[y, :, rows], ag_b.at[x, :, rows]
+            cp_a = remote(part_a, part_a, ag_s.at[t, 2, d], ag_r.at[t, 2, d], dev(dy=d))
+            cp_b = remote(part_b, part_b, ag_s.at[t, 3, d], ag_r.at[t, 3, d], dev(dx=d))
+            cp_a.start()
+            cp_b.start()
+            group += [cp_a, cp_b]
+        ag2.append(group)
 
     e_row = lax.broadcasted_iota(jnp.int32, (8, 128), 0)
     e_lane = lax.broadcasted_iota(jnp.int32, (8, 128), 1)
@@ -274,9 +320,9 @@
     same = (row_of >> 4) == (slot_i >> 1)
     sign = jnp.where((slot_i & 1) == 0, 1.0, -1.0).astype(F32)
 
-    def select(t, carry):
-        rows = pl.ds(pl.multiple_of(t * 16, 16), 16)
-        dst = pl.ds(pl.multiple_of((t % 2) * 32, 32), 32)
+    def select(t):
+        rows = slice(t * 16, t * 16 + 16)
+        dst = slice((t % 2) * 32, (t % 2) * 32 + 32)
         aux = ag_a[:, :, rows, 1024:1152].reshape(256, 128)
         code = dot_nt(pick, aux)
         signed = jnp.where(same, code[:, None, :] * sign, 0.0)
@@ -294,43 +340,66 @@
             )
             got = dot(place, part)
             ssend[:, t // 2, dst, n * 512 + 1024:n * 512 + 1536] = got.astype(BF).reshape(8, 32, 512)
-        return carry
-
-    lax.fori_loop(0, 4, select, 0)
 
     column_devs = [(dz, dc) for dz in (1, 3, 2, 0) for dc in (0, 1)]
+    def send_slots(t):
+        group = []
+        for dz, dc in column_devs:
+            i = dz * 2 + dc
+            to = ((z + dz) % 4) * 2 + (c + dc) % 2
+            rows = pl.ds((t % 2) * 32, 32)
+            src, dst = ssend.at[to, t // 2, rows], srecv.at[me, t // 2, rows]
+            if i == 0:
+                cp = pltpu.make_async_copy(src, dst, z_r.at[t, i])
+            else:
+                cp = remote(src, dst, z_s.at[t, i], z_r.at[t, i], dev(dz=dz, dc=dc))
+            cp.start()
+            group.append(cp)
+        return group
+
     dispatch = []
-    for dz, dc in column_devs:
-        i = dz * 2 + dc
-        to = ((z + dz) % 4) * 2 + (c + dc) % 2
-        if i == 0:
-            cp = pltpu.make_async_copy(ssend.at[me], srecv.at[me], z_r.at[i])
-        else:
-            cp = remote(ssend.at[to], srecv.at[me], z_s.at[i], z_r.at[i], dev(dz=dz, dc=dc))
-        cp.start()
-        dispatch.append(cp)
+    for t in range(4):
+        for cp in ag2[t]:
+            cp.wait()
+        if t == 1:
+            wait_group(first[0])
+            g2 = second(0, None)
+        if t == 2:
+            wait_group(first[1])
+            u2 = second(1, None)
+        select(t)
+        dispatch.append(send_slots(t))
+
     wait_group(g2)
+    first.append(leg_one(2))
     wait_group(u2)
-    for cp in dispatch:
-        cp.wait()
-
-    def hide(i, carry):
-        rows = srecv[pl.ds(i * 2, 2)].reshape(256, 2048)
+
+    for t in range(4):
+        for cp in dispatch[t]:
+            cp.wait()
+
+    def hide_loop(t, carry):
+        half = pl.ds(pl.multiple_of((t % 2) * 32, 32), 32)
+        rows = srecv[:, t // 2, half, :].reshape(256, 2048)
         gate = dot(rows, wgu[0].reshape(2048, 768))
         up = dot(rows, wgu[1].reshape(2048, 768))
-        ag_b[i, :, :, 0:768] = (jax.nn.silu(gate) * up).astype(BF).reshape(4, 64, 768)
+        ag_b[t, :, :, 0:768] = (jax.nn.silu(gate) * up).astype(BF).reshape(4, 64, 768)
         return carry
 
-    lax.fori_loop(0, 4, hide, 0)
+    lax.fori_loop(0, 2, hide_loop, 0)
+    wait_group(first[2])
+    d2 = [second(2, k) for k in range(4)]
+    lax.fori_loop(2, 4, hide_loop, 0)
 
     def down(k):
         cols = slice(k * 512, (k + 1) * 512)
         wait_group(d2[k])
 
-        def tile(i, carry):
-            hidden = ag_b[i, :, :, 0:768].reshape(256, 768)
+        def tile(t, carry):
+            half = pl.ds(pl.multiple_of((t % 2) * 32, 32), 32)
+            hidden = ag_b[t, :, :, 0:768].reshape(256, 768)
             got = dot_nt(hidden, wd[k].reshape(512, 768))
-            srecv[pl.ds(i * 2, 2), :, :, cols] = got.astype(BF).reshape(2, 2, 64, 512)
+            srecv[:, t // 2, half, cols] = got.astype(BF).reshape(8, 32, 512)
             return carry
 
         lax.fori_loop(0, 4, tile, 0)
@@ -403,11 +472,12 @@
         for d in (1, 3, 2):
             xd, yd = (x + d) % 4, (y + d) % 4
             cp_a = remote(
-                ag_a.at[k, xd, :, pl.ds(0, 256)], rs2.at[k, 0, d - 1],
+                ag_a.at[k, xd, :, pl.ds(0, 256)], rs2.at[d - 1, :, pl.ds(k * 512, 256)],
                 r2_s.at[k, 0, d - 1], r2_r.at[k, 0, d - 1], dev(dx=d),
             )
             cp_b = remote(
-                ag_a.at[k, yd, :, pl.ds(256, 256)], rs2.at[k, 1, d - 1],
+                ag_a.at[k, yd, :, pl.ds(256, 256)],
+                rs2.at[d - 1, :, pl.ds(k * 512 + 256, 256)],
                 r2_s.at[k, 1, d - 1], r2_r.at[k, 1, d - 1], dev(dy=d),
             )
             cp_a.start()
@@ -423,8 +493,9 @@
             mine = (x, y)[route]
             total = ag_a[k, mine, :, route * 256:(route + 1) * 256].astype(F32)
             for d in range(3):
-                total = total + rs2[k, route, d].astype(F32)
-            mix[:, k * 512 + route * 256:k * 512 + (route + 1) * 256] = total
+                total = total + rs2[d, :, k * 512 + route * 256:k * 512 + (route + 1) * 256].astype(F32)
+            for i in range(2):
+                o_s[k * 4 + route * 2 + i] = total[:, i * 128:(i + 1) * 128].reshape(2, 32, 128)
 
     backs, sums, ends = {}, {}, {}
     for k in range(7):
@@ -442,7 +513,7 @@
     perm = (o_i == ((p_i >> 4) & 7) * 64 + (p_i >> 7) * 16 + (p_i & 15)).astype(F32).astype(BF)
     for g in range(4):
         v = jnp.concatenate(
-            [mix[:, k * 512 + g * 128:k * 512 + (g + 1) * 128] for k in range(4)], axis=1
+            [o_s[k * 4 + g].reshape(64, 128) for k in range(4)], axis=1
         )
         hi = v.astype(BF)
         lo = (v - hi.astype(F32)).astype(BF)
@@ -457,10 +528,6 @@
     inputs, cache_keys, cache_values, lengths, new_keys, new_values, queries, out_weight,
     norm_gain, router, experts, master_gate, master_up, master_down,
 ):
-    q = queries.reshape(4, 16, 2, 8, 128).transpose(1, 2, 0, 3, 4).reshape(16, 2, 32, 128)
-    nk = jnp.pad(new_keys.transpose(1, 0, 2), ((0, 0), (0, 12), (0, 0)))
-    nv = jnp.pad(new_values.transpose(1, 0, 2), ((0, 0), (0, 12), (0, 0)))
-    lens = jnp.broadcast_to(lengths[:, None, None], (16, 1, 128))
     vm = pl.BlockSpec(memory_space=pltpu.VMEM)
     anyspace = pl.BlockSpec(memory_space=pl.ANY)
     dma = pltpu.SemaphoreType.DMA
@@ -468,7 +535,7 @@
     out = pl.pallas_call(
         kernel,
         out_shape=jax.ShapeDtypeStruct((64, 2048), F32),
-        in_specs=[vm] * 10 + [anyspace] * 4,
+        in_specs=[vm] * 9 + [pl.BlockSpec(memory_space=pltpu.SMEM)] + [anyspace] * 4,
         out_specs=vm,
         scratch_shapes=[
             pltpu.VMEM((DEPTH, 2, 64, 768), F32),
@@ -483,30 +550,32 @@
             pltpu.VMEM((8, 2, 64, 2048), BF),
             pltpu.VMEM((8, 2, 64, 2048), BF),
             pltpu.VMEM((16, 2, 32, 128), F32),
+            pltpu.VMEM((16, 8, 256), F32),
+            pltpu.VMEM((16, 8, 256), F32),
             pltpu.VMEM((64, 2048), BF),
+            pltpu.VMEM((4, 64, 512), BF),
             pltpu.VMEM((64, 2048), F32),
             pltpu.VMEM((4, 256, 256), BF),
             pltpu.VMEM((4, 2, 3, 2, 2, 64, 256), BF),
-            pltpu.VMEM((4, 2, 3, 64, 256), BF),
-            pltpu.VMEM((64, 2048), F32),
+            pltpu.VMEM((3, 64, 2048), BF),
             dma((DEPTH,)),
             dma((3, 2, 8)), dma((3, 2, 8)),
             dma((2, 2, 4)), dma((2, 2, 4)),
             dma((4, 2, 4)), dma((4, 2, 4)),
-            dma, dma((3,)), dma((3,)), dma((3,)), dma((3,)),
-            dma((4, 4)), dma((4, 4)),
-            dma((8,)), dma((8,)),
+            dma, dma((3,)), dma((3,)), dma((3,)), dma((3,)), dma,
+            dma((4, 4, 4)), dma((4, 4, 4)),
+            dma((4, 8)), dma((4, 8)),
             dma((4, 8)), dma((4, 8)),
             dma((4, 2, 3)), dma((4, 2, 3)),
             dma((4, 2, 3)), dma((4, 2, 3)),
         ],
         compiler_params=pltpu.CompilerParams(
-            collective_id=0, has_side_effects=True, vmem_limit_bytes=65_900_000
+            collective_id=0, has_side_effects=True, vmem_limit_bytes=66_900_000
         ),
         name="moe_decode",
     )(
-        inputs.reshape(64, 2048), q, cache_keys, cache_values, nk, nv, lens,
-        norm_gain.reshape(1, 2048), router, experts.reshape(64, 8),
+        inputs.reshape(64, 2048), queries, cache_keys, cache_values, new_keys, new_values,
+        norm_gain, router, experts.transpose(0, 2, 1), lengths,
         out_weight.reshape(4, 2, 64, 2048),
         master_gate.reshape(shape5), master_up.reshape(shape5), master_down.reshape(shape5),
     )

time: 264 us -> 207 us (0.78)
  Pallas kernels: 253 us -> 205 us
  local copies, waits for them, and re-layouts: 8.64 us -> 0 us
    pallas_call x1, Pallas kernels: 253 us -> 205 us  [per_device(): pl.pallas_call(kernel, out_shape=jax.ShapeDtypeStruct((64, 2048), F32), i...]
    unnamed x4 -> x0, local copies, waits for them, and re-layouts: 3.93 us -> none
where the time goes in v1:
time: 207 us
  Pallas kernels  205 us (99%)
    pallas_call x1, Pallas kernels, per_device(): pl.pallas_call(kernel, out_shape=jax.ShapeDtypeStruct((64, 2048), F32), i...  205 us

profile of v1, /device:TPU:0, one launch (start us, length us, event | category | flops | bytes accessed | tf_op | source)
XLA Modules:
  0.0 207.1 jit_solution(16532482715596693406)
XLA Ops:
  0.0 205.3 %moe_decode.1 = f32[64,2048]{1,0:T(8,128)} custom-call(bf16[64,2048]{1,0:T(8,128)(2,1)} %bitcast.11, bf16[4,16,2048]{2,1,0:T(8,128)(2,1)} %q_ref.1, bf16[16,128,256]{2,1,0:T(8,128)(2,1)} %ck_ref.1, bf16[16,128,256]{2,1,0:T(8,128)(2,1)} %cv_ref.1, bf16[4,16,256]{2,1,0:T(8,128)(2,1)} %nk_ref.1, bf16[4,16,256]{2,1,0:T(8,128)(2,1)} %nv_ref.1, ...), custom_call_target="tpu_custom_call" | custom-call | tf_op jit(solution)/shard_map/moe_decode/pallas_call | solution.py:535
  205.3 1.8 convert_element_type.3

commit v2 on v1

--- a/solution.py
+++ b/solution.py
@@ -30,12 +30,12 @@
 
 
 def kernel(
-    x_ref, q_ref, ck_ref, cv_ref, nk_ref, nv_ref, gain_ref, router_ref, ids_ref, len_ref,
-    wo_ref, mg_ref, mu_ref, md_ref,
+    x_ref, q_ref, nk_ref, nv_ref, gain_ref, ids_ref, len_ref,
+    ck_hbm, cv_hbm, router_hbm, wo_ref, mg_ref, mu_ref, md_ref,
     out_ref,
-    stage, ws, mid_a, mid_b, wgu, wd, wout, ag_a, ag_b, ssend, srecv,
+    ck_ref, cv_ref, router_ref, stage, ws, mid_a, mid_b, wgu, wd, wout, ag_a, ag_b, ssend, srecv,
     o_s, nk_s, nv_s, att, attr, resid, pg, rs1, rs2,
-    st_sem, w1_s, w1_r, w2_s, w2_r, d2_s, d2_r, own_sem, o_snd, o_rcv, f_snd, f_rcv, one_sem,
+    st_sem, in_sem, w1_s, w1_r, d1_s, d1_r, w2_s, w2_r, d2_s, d2_r, own_sem, o_snd, o_rcv, f_snd, f_rcv, one_sem,
     ag_s, ag_r, z_s, z_r, t_s, t_r, r1_s, r1_r, r2_s, r2_r,
 ):
     z = lax.axis_index("fsdp")
@@ -66,6 +66,14 @@
         load(0, j, j).start()
     own_out = pltpu.make_async_copy(wo_ref, wout.at[pl.ds(0, 4)], own_sem)
     own_out.start()
+    local_ins = [
+        pltpu.make_async_copy(src, dst, in_sem.at[i])
+        for i, (src, dst) in enumerate(
+            ((ck_hbm, ck_ref), (cv_hbm, cv_ref), (router_hbm, router_ref))
+        )
+    ]
+    for cp in local_ins:
+        cp.start()
 
     partners = [(d, 0, k, 0) for d in (1, 2, 3) for k in (0, 1)]
     partners += [(0, d, k, 0) for d in (1, 2, 3) for k in (0, 1)]
@@ -98,25 +106,26 @@
         lax.fori_loop(0, 16 - DEPTH, step_a, 0)
         lax.fori_loop(16 - DEPTH, 16, step_b, 0)
 
-    def leg_one(t):
-        group = []
+    def leg_one(t, k=None):
+        group = []
+        snd, rcv = (w1_s.at[t], w1_r.at[t]) if k is None else (d1_s.at[k], d1_r.at[k])
+        rows = pl.ds(0, 64) if k is None else pl.ds(k * 16, 16)
         for d in (1, 3, 2, 0):
             for dc in (0, 1):
                 i = d * 2 + dc
                 xd, yd, cd = (x + d) % 4, (y + d) % 4, (c + dc) % 2
-                src_a = ws.at[t, xd, :, cd, :, pl.ds(0, 384)]
-                src_b = ws.at[t, :, yd, cd, :, pl.ds(384, 384)]
+                src_a = ws.at[t, xd, :, cd, rows, pl.ds(0, 384)]
+                src_b = ws.at[t, :, yd, cd, rows, pl.ds(384, 384)]
+                dst_a, dst_b = mid_a.at[t, x, c, :, rows], mid_b.at[t, y, c, :, rows]
                 if i == 0:
-                    cp_a = pltpu.make_async_copy(src_a, mid_a.at[t, x, c], w1_r.at[t, 0, i])
-                    cp_b = pltpu.make_async_copy(src_b, mid_b.at[t, y, c], w1_r.at[t, 1, i])
+                    cp_a = pltpu.make_async_copy(src_a, dst_a, rcv.at[0, i])
+                    cp_b = pltpu.make_async_copy(src_b, dst_b, rcv.at[1, i])
                 else:
                     cp_a = remote(
-                        src_a, mid_a.at[t, x, c], w1_s.at[t, 0, i], w1_r.at[t, 0, i],
-                        dev(dx=d, dc=dc),
+                        src_a, dst_a, snd.at[0, i], rcv.at[0, i], dev(dx=d, dc=dc)
                     )
                     cp_b = remote(
-                        src_b, mid_b.at[t, y, c], w1_s.at[t, 1, i], w1_r.at[t, 1, i],
-                        dev(dy=d, dc=dc),
+                        src_b, dst_b, snd.at[1, i], rcv.at[1, i], dev(dy=d, dc=dc)
                     )
                     drains.extend([cp_a, cp_b])
                 cp_a.start()
@@ -160,12 +169,15 @@
 
     cast(0)
     first = [leg_one(0)]
-    cast(1)
-    first.append(leg_one(1))
+    for cp in local_ins:
+        cp.wait()
 
     inv = 1.0 / math.sqrt(128.0)
     neg = -jnp.inf
-    lane = lax.broadcasted_iota(jnp.int32, (32, 128), 1)
+    lane = lax.broadcasted_iota(jnp.int32, (32, 136), 1)
+    fresh_ok = (lane >= 128) & (
+        lane - 128 <= (lax.broadcasted_iota(jnp.int32, (32, 136), 0) >> 3)
+    )
     for g in range(2):
         for h in range(8):
             for t in range(4):
@@ -178,24 +190,17 @@
         else:
             nk_s[:, s, :] = jnp.zeros((16, 256), F32)
             nv_s[:, s, :] = jnp.zeros((16, 256), F32)
-    fresh_ok = lax.broadcasted_iota(jnp.int32, (32, 8), 1) <= (
-        lax.broadcasted_iota(jnp.int32, (32, 8), 0) >> 3
-    )
-
     def attend(r, carry):
-        ok = lane < len_ref[r]
+        ok = fresh_ok | (lane < len_ref[r])
         for g in range(2):
             cols = slice(g * 128, (g + 1) * 128)
             qq = o_s[r, g].astype(BF)
-            s = jnp.where(ok, dot_nt(qq, ck_ref[r, :, cols]) * inv, neg)
-            f = jnp.where(fresh_ok, dot_nt(qq, nk_s[r, :, cols].astype(BF)) * inv, neg)
-            top = jnp.maximum(
-                jnp.max(s, axis=-1, keepdims=True), jnp.max(f, axis=-1, keepdims=True)
-            )
-            es, ef = jnp.exp(s - top), jnp.exp(f - top)
-            total = jnp.sum(es, axis=-1, keepdims=True) + jnp.sum(ef, axis=-1, keepdims=True)
-            ps, pf = (es / total).astype(BF), (ef / total).astype(BF)
-            o_s[r, g] = dot(ps, cv_ref[r, :, cols]) + dot(pf, nv_s[r, :, cols].astype(BF))
+            keys = jnp.concatenate([ck_ref[r, :, cols], nk_s[r, :, cols].astype(BF)], axis=0)
+            values = jnp.concatenate([cv_ref[r, :, cols], nv_s[r, :, cols].astype(BF)], axis=0)
+            s = jnp.where(ok, dot_nt(qq, keys) * inv, neg)
+            es = jnp.exp(s - jnp.max(s, axis=-1, keepdims=True))
+            ps = (es / jnp.sum(es, axis=-1, keepdims=True)).astype(BF)
+            o_s[r, g] = dot(ps, values)
         return carry
 
     def attend_some(i, carry):
@@ -223,6 +228,8 @@
         att.at[:, pl.ds(pl.multiple_of(z * 512, 512), 512)], attr.at[z], one_sem
     )
     mine.start()
+    cast(1)
+    first.append(leg_one(1))
     mine.wait()
     own_out.wait()
     for cp in toward:
@@ -297,13 +304,14 @@
             cp_b.start()
             group += [cp_a, cp_b]
         ag1.append(group)
-    ag2 = []
-    for t in range(4):
+    ag2, ag3 = [], []
+
+    def gather_two(t):
         rows = pl.ds(t * 16, 16)
         for cp in ag1[t]:
             cp.wait()
         group = []
-        for d in (1, 3, 2):
+        for d in (1, 3):
             part_a, part_b = ag_a.at[y, :, rows], ag_b.at[x, :, rows]
             cp_a = remote(part_a, part_a, ag_s.at[t, 2, d], ag_r.at[t, 2, d], dev(dy=d))
             cp_b = remote(part_b, part_b, ag_s.at[t, 3, d], ag_r.at[t, 3, d], dev(dx=d))
@@ -311,6 +319,22 @@
             cp_b.start()
             group += [cp_a, cp_b]
         ag2.append(group)
+
+    def gather_three(t):
+        rows = pl.ds(t * 16, 16)
+        for cp in ag2[t]:
+            cp.wait()
+        group = []
+        for i, d in ((0, 1), (2, 3)):
+            half = pl.ds(i, 2)
+            part_a = ag_a.at[(y + 4 - d) % 4, half, rows]
+            part_b = ag_b.at[(x + 4 - d) % 4, half, rows]
+            cp_a = remote(part_a, part_a, ag_s.at[t, 2, i], ag_r.at[t, 2, i], dev(dy=d))
+            cp_b = remote(part_b, part_b, ag_s.at[t, 3, i], ag_r.at[t, 3, i], dev(dx=d))
+            cp_a.start()
+            cp_b.start()
+            group += [cp_a, cp_b]
+        ag3.append(group)
 
     e_row = lax.broadcasted_iota(jnp.int32, (8, 128), 0)
     e_lane = lax.broadcasted_iota(jnp.int32, (8, 128), 1)
@@ -358,21 +382,31 @@
         return group
 
     dispatch = []
-    for t in range(4):
-        for cp in ag2[t]:
-            cp.wait()
-        if t == 1:
+    for step in range(6):
+        if step < 4:
+            gather_two(step)
+        if 1 <= step < 5:
+            gather_three(step - 1)
+        if step == 4:
             wait_group(first[0])
             g2 = second(0, None)
-        if t == 2:
-            wait_group(first[1])
-            u2 = second(1, None)
-        select(t)
-        dispatch.append(send_slots(t))
-
+        if step >= 2:
+            t = step - 2
+            for cp in ag3[t]:
+                cp.wait()
+            if t == 2:
+                wait_group(first[1])
+                u2 = second(1, None)
+            select(t)
+            dispatch.append(send_slots(t))
+
+    d1 = [leg_one(2, 0)]
     wait_group(g2)
-    first.append(leg_one(2))
+    d1.append(leg_one(2, 1))
+    wait_group(d1[0])
+    d2 = [second(2, 0)]
     wait_group(u2)
+    d1.append(leg_one(2, 2))
 
     for t in range(4):
         for cp in dispatch[t]:
@@ -387,8 +421,9 @@
         return carry
 
     lax.fori_loop(0, 2, hide_loop, 0)
-    wait_group(first[2])
-    d2 = [second(2, k) for k in range(4)]
+    wait_group(d1[1])
+    d2.append(second(2, 1))
+    d1.append(leg_one(2, 3))
     lax.fori_loop(2, 4, hide_loop, 0)
 
     def down(k):
@@ -501,6 +536,9 @@
     for k in range(7):
         if k < 4:
             backs[k] = down(k)
+        if k < 2:
+            wait_group(d1[k + 2])
+            d2.append(second(2, k + 2))
         if 0 <= k - 1 < 4:
             sums[k - 1] = combine(k - 1, backs[k - 1])
         if 0 <= k - 2 < 4:
@@ -535,9 +573,12 @@
     out = pl.pallas_call(
         kernel,
         out_shape=jax.ShapeDtypeStruct((64, 2048), F32),
-        in_specs=[vm] * 9 + [pl.BlockSpec(memory_space=pltpu.SMEM)] + [anyspace] * 4,
+        in_specs=[vm] * 6 + [pl.BlockSpec(memory_space=pltpu.SMEM)] + [anyspace] * 7,
         out_specs=vm,
         scratch_shapes=[
+            pltpu.VMEM((16, 128, 256), BF),
+            pltpu.VMEM((16, 128, 256), BF),
+            pltpu.VMEM((2048, 128), BF),
             pltpu.VMEM((DEPTH, 2, 64, 768), F32),
             pltpu.VMEM((3, 4, 4, 2, 64, 768), BF),
             pltpu.VMEM((3, 4, 2, 4, 64, 384), BF),
@@ -559,7 +600,7 @@
             pltpu.VMEM((4, 2, 3, 2, 2, 64, 256), BF),
             pltpu.VMEM((3, 64, 2048), BF),
             dma((DEPTH,)),
-            dma((3, 2, 8)), dma((3, 2, 8)),
+            dma((3,)), dma((2, 2, 8)), dma((2, 2, 8)), dma((4, 2, 8)), dma((4, 2, 8)),
             dma((2, 2, 4)), dma((2, 2, 4)),
             dma((4, 2, 4)), dma((4, 2, 4)),
             dma, dma((3,)), dma((3,)), dma((3,)), dma((3,)), dma,
@@ -574,8 +615,8 @@
         ),
         name="moe_decode",
     )(
-        inputs.reshape(64, 2048), queries, cache_keys, cache_values, new_keys, new_values,
-        norm_gain, router, experts.transpose(0, 2, 1), lengths,
+        inputs.reshape(64, 2048), queries, new_keys, new_values,
+        norm_gain, experts.transpose(0, 2, 1), lengths, cache_keys, cache_values, router,
         out_weight.reshape(4, 2, 64, 2048),
         master_gate.reshape(shape5), master_up.reshape(shape5), master_down.reshape(shape5),
     )

time: 207 us -> 192 us (0.928)
  Pallas kernels: 205 us -> 190 us
    pallas_call x1, Pallas kernels: 205 us -> 190 us  [per_device(): pl.pallas_call(kernel, out_shape=jax.ShapeDtypeStruct((64, 2048), F32), i...]
where the time goes in v2:
time: 192 us
  Pallas kernels  190 us (99%)
    pallas_call x1, Pallas kernels, per_device(): pl.pallas_call(kernel, out_shape=jax.ShapeDtypeStruct((64, 2048), F32), i...  190 us

profile of v2, /device:TPU:0, one launch (start us, length us, event | category | flops | bytes accessed | tf_op | source)
XLA Modules:
  0.0 192.2 jit_solution(4608002353771857582)
XLA Ops:
  0.0 190.4 %moe_decode.1 = f32[64,2048]{1,0:T(8,128)} custom-call(bf16[64,2048]{1,0:T(8,128)(2,1)} %bitcast.11, bf16[4,16,2048]{2,1,0:T(8,128)(2,1)} %q_ref.1, bf16[4,16,256]{2,1,0:T(8,128)(2,1)} %nk_ref.1, bf16[4,16,256]{2,1,0:T(8,128)(2,1)} %nv_ref.1, bf16[2048]{0:T(1024)(128)(2,1)} %gain_ref.1, s32[4,8,16]{2,1,0:T(8,128)} %bitcast.12, s32[16]{0:T(128)} %len_ref.1, ...), custom_call_target="tpu_custom_call" | custom-call | tf_op jit(solution)/shard_map/moe_decode/pallas_call | solution.py:573
  190.4 1.8 convert_element_type.3

commit v3 on v2

--- a/solution.py
+++ b/solution.py
@@ -15,6 +15,7 @@
 TN = (((0,), (0,)), ((), ()))
 DEPTH = 8
 UNROLL = 4
+G_AT, U_AT = 5, 5
 
 
 def dot(a, b):
@@ -110,7 +111,7 @@
         group = []
         snd, rcv = (w1_s.at[t], w1_r.at[t]) if k is None else (d1_s.at[k], d1_r.at[k])
         rows = pl.ds(0, 64) if k is None else pl.ds(k * 16, 16)
-        for d in (1, 3, 2, 0):
+        for d in (2, 1, 3, 0):
             for dc in (0, 1):
                 i = d * 2 + dc
                 xd, yd, cd = (x + d) % 4, (y + d) % 4, (c + dc) % 2
@@ -142,7 +143,7 @@
 
     def second(t, k):
         group = []
-        for d in (1, 3, 2, 0):
+        for d in (2, 1, 3, 0):
             xd, yd = (x + d) % 4, (y + d) % 4
             if k is None:
                 src_a, src_b = mid_a.at[t, :, :, yd], mid_b.at[t, :, :, xd]
@@ -169,6 +170,8 @@
 
     cast(0)
     first = [leg_one(0)]
+    cast(1)
+    first.append(leg_one(1))
     for cp in local_ins:
         cp.wait()
 
@@ -228,8 +231,6 @@
         att.at[:, pl.ds(pl.multiple_of(z * 512, 512), 512)], attr.at[z], one_sem
     )
     mine.start()
-    cast(1)
-    first.append(leg_one(1))
     mine.wait()
     own_out.wait()
     for cp in toward:
@@ -243,13 +244,17 @@
 
     lax.fori_loop(0, 4, project, 0)
     partial = []
-    for dz in (1, 3, 2):
-        cp = remote(
-            ssend.at[(z + dz) % 4, 0], rs2.at[dz - 1], f_snd.at[dz - 1], f_rcv.at[dz - 1],
-            dev(dz=dz),
-        )
-        cp.start()
-        partial.append(cp)
+    for t in range(4):
+        rows = pl.ds(t * 16, 16)
+        group = []
+        for dz in (1, 3, 2):
+            cp = remote(
+                ssend.at[(z + dz) % 4, 0, rows], rs2.at[dz - 1, rows],
+                f_snd.at[t, dz - 1], f_rcv.at[t, dz - 1], dev(dz=dz),
+            )
+            cp.start()
+            group.append(cp)
+        partial.append(group)
 
     def project_own(n, carry):
         cols = pl.ds(pl.multiple_of(n * 512, 512), 512)
@@ -259,44 +264,40 @@
 
     lax.fori_loop(0, 4, project_own, 0)
     cast(2)
-    for cp in partial:
-        cp.wait()
-    for n in range(4):
-        cols = slice(n * 512, (n + 1) * 512)
-        total = resid[:, cols]
+
+    expert_i = lax.broadcasted_iota(jnp.int32, (128, 16), 0)
+    row_i = lax.broadcasted_iota(jnp.int32, (16, 16), 0)
+    col_i = lax.broadcasted_iota(jnp.int32, (16, 16), 1)
+    eye = (row_i == col_i).astype(F32).astype(BF)
+    before = (col_i < row_i).astype(F32).astype(BF)
+    gain = gain_ref[...].astype(F32).reshape(1, 2048)
+    ag1 = []
+
+    def gather_one(t):
+        for cp in partial[t]:
+            cp.wait()
+        span = slice(t * 16, t * 16 + 16)
+        res = resid[span, :]
         for d in range(3):
-            total = total + rs2[d, :, cols].astype(F32)
-        resid[:, cols] = total
-    res = resid[...]
-    mean_square = jnp.mean(res * res, axis=-1, keepdims=True)
-    normed = (res * lax.rsqrt(mean_square + 1e-06) * gain_ref[...].astype(F32).reshape(1, 2048)).astype(BF)
-    ag_a[y, x, :, 0:1024] = normed[:, 0:1024]
-    ag_b[x, y] = normed[:, 1024:2048]
-    logits = dot(normed, router_ref[...])
-    expert_i = lax.broadcasted_iota(jnp.int32, (128, 16), 0)
-    eye_r = lax.broadcasted_iota(jnp.int32, (64, 16), 0)
-    eye_c = lax.broadcasted_iota(jnp.int32, (64, 16), 1)
-    member = jnp.zeros((64, 128), F32)
-    for t in range(4):
+            res = res + rs2[d, span, :].astype(F32)
+        resid[span, :] = res
+        mean_square = jnp.mean(res * res, axis=-1, keepdims=True)
+        normed = (res * lax.rsqrt(mean_square + 1e-06) * gain).astype(BF)
+        ag_a[y, x, span, 0:1024] = normed[:, 0:1024]
+        ag_b[x, y, span, :] = normed[:, 1024:2048]
+        logits = dot(normed, router_ref[...])
         named = jnp.zeros((128, 16), F32)
         for k in range(8):
             named = named + (ids_ref[t, k:k + 1, :] == expert_i).astype(F32)
-        eye = (eye_r == eye_c + t * 16).astype(F32).astype(BF)
-        member = member + dot_nt(eye, named.astype(BF))
-    row_i = lax.broadcasted_iota(jnp.int32, (64, 64), 0)
-    col_i = lax.broadcasted_iota(jnp.int32, (64, 64), 1)
-    before = ((row_i >> 4) == (col_i >> 4)) & (col_i < row_i)
-    rank = dot(before.astype(F32).astype(BF), member.astype(BF))
-    chosen = jnp.where(member > 0.5, logits, neg)
-    chosen_exp = jnp.exp(chosen - jnp.max(chosen, axis=-1, keepdims=True))
-    gates = chosen_exp / jnp.sum(chosen_exp, axis=-1, keepdims=True)
-    ag_a[y, x, :, 1024:1152] = jnp.where(rank < 0.5, gates, -gates).astype(BF)
-
-    ag1 = []
-    for t in range(4):
+        member = dot_nt(eye, named.astype(BF))
+        rank = dot(before, member.astype(BF))
+        chosen = jnp.where(member > 0.5, logits, neg)
+        chosen_exp = jnp.exp(chosen - jnp.max(chosen, axis=-1, keepdims=True))
+        gates = chosen_exp / jnp.sum(chosen_exp, axis=-1, keepdims=True)
+        ag_a[y, x, span, 1024:1152] = jnp.where(rank < 0.5, gates, -gates).astype(BF)
         rows = pl.ds(t * 16, 16)
         group = []
-        for d in (1, 3, 2):
+        for d in (2, 1, 3):
             part_a, part_b = ag_a.at[y, x, rows], ag_b.at[x, y, rows]
             cp_a = remote(part_a, part_a, ag_s.at[t, 0, d], ag_r.at[t, 0, d], dev(dx=d))
             cp_b = remote(part_b, part_b, ag_s.at[t, 1, d], ag_r.at[t, 1, d], dev(dy=d))
@@ -365,7 +366,7 @@
             got = dot(place, part)
             ssend[:, t // 2, dst, n * 512 + 1024:n * 512 + 1536] = got.astype(BF).reshape(8, 32, 512)
 
-    column_devs = [(dz, dc) for dz in (1, 3, 2, 0) for dc in (0, 1)]
+    column_devs = [(dz, dc) for dz in (2, 1, 3, 0) for dc in (0, 1)]
     def send_slots(t):
         group = []
         for dz, dc in column_devs:
@@ -382,19 +383,21 @@
         return group
 
     dispatch = []
-    for step in range(6):
+    for step in range(7):
         if step < 4:
-            gather_two(step)
+            gather_one(step)
         if 1 <= step < 5:
-            gather_three(step - 1)
-        if step == 4:
+            gather_two(step - 1)
+        if 2 <= step < 6:
+            gather_three(step - 2)
+        if step == G_AT:
             wait_group(first[0])
             g2 = second(0, None)
-        if step >= 2:
-            t = step - 2
+        if step >= 3:
+            t = step - 3
             for cp in ag3[t]:
                 cp.wait()
-            if t == 2:
+            if step == U_AT:
                 wait_group(first[1])
                 u2 = second(1, None)
             select(t)
@@ -426,9 +429,13 @@
     d1.append(leg_one(2, 3))
     lax.fori_loop(2, 4, hide_loop, 0)
 
-    def down(k):
+    pieces = ((0, 0, 4), (1, 0, 4), (2, 0, 4), (3, 0, 2), (3, 2, 2))
+
+    def down(p):
+        k, t0, nt = pieces[p]
         cols = slice(k * 512, (k + 1) * 512)
-        wait_group(d2[k])
+        if t0 == 0:
+            wait_group(d2[k])
 
         def tile(t, carry):
             half = pl.ds(pl.multiple_of((t % 2) * 32, 32), 32)
@@ -437,19 +444,20 @@
             srecv[:, t // 2, half, cols] = got.astype(BF).reshape(8, 32, 512)
             return carry
 
-        lax.fori_loop(0, 4, tile, 0)
+        lax.fori_loop(t0, t0 + nt, tile, 0)
+        part = pl.ds(t0 // 2, nt // 2)
         group = []
         for dz, dc in column_devs:
             i = dz * 2 + dc
             to = ((z + dz) % 4) * 2 + (c + dc) % 2
-            dst = wout.at[me, :, :, pl.ds(k * 512, 512)]
+            dst = wout.at[me, part, :, pl.ds(k * 512, 512)]
             if i == 0:
                 cp = pltpu.make_async_copy(
-                    srecv.at[me, :, :, pl.ds(k * 512, 512)], dst, t_r.at[k, i]
+                    srecv.at[me, part, :, pl.ds(k * 512, 512)], dst, t_r.at[p, i]
                 )
             else:
                 cp = remote(
-                    srecv.at[to, :, :, pl.ds(k * 512, 512)], dst, t_s.at[k, i], t_r.at[k, i],
+                    srecv.at[to, part, :, pl.ds(k * 512, 512)], dst, t_s.at[p, i], t_r.at[p, i],
                     dev(dz=dz, dc=dc),
                 )
                 drains.append(cp)
@@ -457,7 +465,9 @@
             group.append((i, cp))
         return group
 
-    def combine(k, group):
+    def combine(p, group):
+        k, t0, nt = pieces[p]
+        some = pl.ds(t0 * 16, nt * 16)
         wait_group(group)
 
         def tile(t, carry):
@@ -474,18 +484,19 @@
                     ]
             return carry
 
-        lax.fori_loop(0, 4, tile, 0)
+        lax.fori_loop(t0, t0 + nt, tile, 0)
         sums = []
-        for d in (1, 3, 2):
+        for d in (2, 1, 3):
             xd, yd = (x + d) % 4, (y + d) % 4
             cp_a = remote(
-                wout.at[pl.ds(8 + yd * 2, 2), :, :, pl.ds(k * 512, 256)], rs1.at[k, 0, d - 1],
-                r1_s.at[k, 0, d - 1], r1_r.at[k, 0, d - 1], dev(dy=d),
+                wout.at[pl.ds(8 + yd * 2, 2), :, some, pl.ds(k * 512, 256)],
+                rs1.at[k, 0, d - 1, :, :, some],
+                r1_s.at[p, 0, d - 1], r1_r.at[p, 0, d - 1], dev(dy=d),
             )
             cp_b = remote(
-                wout.at[pl.ds(8 + xd * 2, 2), :, :, pl.ds(k * 512 + 256, 256)],
-                rs1.at[k, 1, d - 1],
-                r1_s.at[k, 1, d - 1], r1_r.at[k, 1, d - 1], dev(dx=d),
+                wout.at[pl.ds(8 + xd * 2, 2), :, some, pl.ds(k * 512 + 256, 256)],
+                rs1.at[k, 1, d - 1, :, :, some],
+                r1_s.at[p, 1, d - 1], r1_r.at[p, 1, d - 1], dev(dx=d),
             )
             cp_a.start()
             cp_b.start()
@@ -493,27 +504,31 @@
         drains.extend(sums)
         return sums
 
-    def halfway(k, sums):
+    def halfway(p, sums):
+        k, t0, nt = pieces[p]
+        n = nt * 16
+        span, some = slice(t0 * 16, t0 * 16 + n), pl.ds(t0 * 16, n)
         for cp in sums:
             cp.wait_recv()
         for route in range(2):
             mine = (y, x)[route]
             lanes = slice(k * 512 + route * 256, k * 512 + route * 256 + 256)
-            total = wout[pl.ds(8 + mine * 2, 2), :, :, lanes].reshape(256, 256).astype(F32)
+            total = wout[pl.ds(8 + mine * 2, 2), :, span, lanes].reshape(4 * n, 256).astype(F32)
             for d in range(3):
-                total = total + rs1[k, route, d].reshape(256, 256).astype(F32)
-            ag_a[k, :, :, route * 256:(route + 1) * 256] = total.astype(BF).reshape(4, 64, 256)
-        group = []
-        for d in (1, 3, 2):
+                total = total + rs1[k, route, d, :, :, span, :].reshape(4 * n, 256).astype(F32)
+            ag_a[k, :, span, route * 256:(route + 1) * 256] = total.astype(BF).reshape(4, n, 256)
+        group = []
+        for d in (2, 1, 3):
             xd, yd = (x + d) % 4, (y + d) % 4
             cp_a = remote(
-                ag_a.at[k, xd, :, pl.ds(0, 256)], rs2.at[d - 1, :, pl.ds(k * 512, 256)],
-                r2_s.at[k, 0, d - 1], r2_r.at[k, 0, d - 1], dev(dx=d),
+                ag_a.at[k, xd, some, pl.ds(0, 256)],
+                rs2.at[d - 1, some, pl.ds(k * 512, 256)],
+                r2_s.at[p, 0, d - 1], r2_r.at[p, 0, d - 1], dev(dx=d),
             )
             cp_b = remote(
-                ag_a.at[k, yd, :, pl.ds(256, 256)],
-                rs2.at[d - 1, :, pl.ds(k * 512 + 256, 256)],
-                r2_s.at[k, 1, d - 1], r2_r.at[k, 1, d - 1], dev(dy=d),
+                ag_a.at[k, yd, some, pl.ds(256, 256)],
+                rs2.at[d - 1, some, pl.ds(k * 512 + 256, 256)],
+                r2_s.at[p, 1, d - 1], r2_r.at[p, 1, d - 1], dev(dy=d),
             )
             cp_a.start()
             cp_b.start()
@@ -521,29 +536,41 @@
         drains.extend(group)
         return group
 
-    def close(k, group):
+    def close(p, group):
+        k, t0, nt = pieces[p]
+        n = nt * 16
+        span = slice(t0 * 16, t0 * 16 + n)
         for cp in group:
             cp.wait_recv()
         for route in range(2):
             mine = (x, y)[route]
-            total = ag_a[k, mine, :, route * 256:(route + 1) * 256].astype(F32)
+            total = ag_a[k, mine, span, route * 256:(route + 1) * 256].astype(F32)
+            cols = slice(k * 512 + route * 256, k * 512 + (route + 1) * 256)
             for d in range(3):
-                total = total + rs2[d, :, k * 512 + route * 256:k * 512 + (route + 1) * 256].astype(F32)
+                total = total + rs2[d, span, cols].astype(F32)
             for i in range(2):
-                o_s[k * 4 + route * 2 + i] = total[:, i * 128:(i + 1) * 128].reshape(2, 32, 128)
+                o_s[k * 4 + route * 2 + i, t0 // 2:(t0 + nt) // 2] = total[
+                    :, i * 128:(i + 1) * 128
+                ].reshape(nt // 2, 32, 128)
 
     backs, sums, ends = {}, {}, {}
-    for k in range(7):
-        if k < 4:
+    for k in range(8):
+        if k == 4:
+            early = drains[:]
+            drains.clear()
+        if k < 5:
             backs[k] = down(k)
         if k < 2:
             wait_group(d1[k + 2])
             d2.append(second(2, k + 2))
-        if 0 <= k - 1 < 4:
+        if k == 4:
+            for cp in early:
+                cp.wait_send()
+        if 0 <= k - 1 < 5:
             sums[k - 1] = combine(k - 1, backs[k - 1])
-        if 0 <= k - 2 < 4:
+        if 0 <= k - 2 < 5:
             ends[k - 2] = halfway(k - 2, sums[k - 2])
-        if 0 <= k - 3 < 4:
+        if 0 <= k - 3 < 5:
             close(k - 3, ends[k - 3])
 
     p_i = lax.broadcasted_iota(jnp.int32, (512, 512), 0)
@@ -557,7 +584,7 @@
         lo = (v - hi.astype(F32)).astype(BF)
         out_ref[:, g * 512:(g + 1) * 512] = (
             resid[:, g * 512:(g + 1) * 512] + dot(hi, perm) + dot(lo, perm)
-        )
+        ).astype(BF)
     for cp in drains:
         cp.wait_send()
 
@@ -572,7 +599,7 @@
     shape5 = (4, 4, 2, 64, 768)
     out = pl.pallas_call(
         kernel,
-        out_shape=jax.ShapeDtypeStruct((64, 2048), F32),
+        out_shape=jax.ShapeDtypeStruct((64, 2048), BF),
         in_specs=[vm] * 6 + [pl.BlockSpec(memory_space=pltpu.SMEM)] + [anyspace] * 7,
         out_specs=vm,
         scratch_shapes=[
@@ -603,12 +630,12 @@
             dma((3,)), dma((2, 2, 8)), dma((2, 2, 8)), dma((4, 2, 8)), dma((4, 2, 8)),
             dma((2, 2, 4)), dma((2, 2, 4)),
             dma((4, 2, 4)), dma((4, 2, 4)),
-            dma, dma((3,)), dma((3,)), dma((3,)), dma((3,)), dma,
+            dma, dma((3,)), dma((3,)), dma((4, 3)), dma((4, 3)), dma,
             dma((4, 4, 4)), dma((4, 4, 4)),
             dma((4, 8)), dma((4, 8)),
-            dma((4, 8)), dma((4, 8)),
-            dma((4, 2, 3)), dma((4, 2, 3)),
-            dma((4, 2, 3)), dma((4, 2, 3)),
+            dma((5, 8)), dma((5, 8)),
+            dma((5, 2, 3)), dma((5, 2, 3)),
+            dma((5, 2, 3)), dma((5, 2, 3)),
         ],
         compiler_params=pltpu.CompilerParams(
             collective_id=0, has_side_effects=True, vmem_limit_bytes=66_900_000
@@ -620,7 +647,7 @@
         out_weight.reshape(4, 2, 64, 2048),
         master_gate.reshape(shape5), master_up.reshape(shape5), master_down.reshape(shape5),
     )
-    return out.astype(BF).reshape(4, 16, 2048)
+    return out.reshape(4, 16, 2048)
 
 
 def solution(mesh):

time: 192 us -> 189 us (0.984)
  Pallas kernels: 190 us -> 187 us
    pallas_call x1, Pallas kernels: 190 us -> 187 us  [per_device(): pl.pallas_call(kernel, out_shape=jax.ShapeDtypeStruct((64, 2048), BF), in...]
where the time goes in v3:
time: 189 us
  Pallas kernels  187 us (99%)
    pallas_call x1, Pallas kernels, per_device(): pl.pallas_call(kernel, out_shape=jax.ShapeDtypeStruct((64, 2048), BF), in...  187 us

profile of v3, /device:TPU:0, one launch (start us, length us, event | category | flops | bytes accessed | tf_op | source)
XLA Modules:
  0.0 189.1 jit_solution(12883368943211592496)
XLA Ops:
  0.0 187.4 %moe_decode.1 = bf16[64,2048]{1,0:T(8,128)(2,1)} custom-call(bf16[64,2048]{1,0:T(8,128)(2,1)} %bitcast.12, bf16[4,16,2048]{2,1,0:T(8,128)(2,1)} %q_ref.1, bf16[4,16,256]{2,1,0:T(8,128)(2,1)} %nk_ref.1, bf16[4,16,256]{2,1,0:T(8,128)(2,1)} %nv_ref.1, bf16[2048]{0:T(1024)(128)(2,1)} %gain_ref.1, s32[4,8,16]{2,1,0:T(8,128)} %bitcast.13, s32[16]{0:T(128)} %len_ref.1, ...), custom_call_target="tpu_custom_call" | custom-call | tf_op jit(solution)/shard_map/moe_decode/pallas_call | solution.py:600
  187.4 1.7 copy.16

commit v4 on v3

--- a/solution.py
+++ b/solution.py
@@ -221,7 +221,7 @@
                 ].astype(BF)
 
     toward = []
-    for dz in (1, 3, 2):
+    for dz in (2, 1, 3):
         to = (z + dz) % 4
         cols = pl.ds(pl.multiple_of(to * 512, 512), 512)
         cp = remote(att.at[:, cols], attr.at[z], o_snd.at[dz - 1], o_rcv.at[dz - 1], dev(dz=dz))
@@ -247,7 +247,7 @@
     for t in range(4):
         rows = pl.ds(t * 16, 16)
         group = []
-        for dz in (1, 3, 2):
+        for dz in (2, 1, 3):
             cp = remote(
                 ssend.at[(z + dz) % 4, 0, rows], rs2.at[dz - 1, rows],
                 f_snd.at[t, dz - 1], f_rcv.at[t, dz - 1], dev(dz=dz),

time: 189 us -> 189 us (level)
  no operation moved by 1% of the time
where the time goes in v4:
time: 189 us
  Pallas kernels  187 us (99%)
    pallas_call x1, Pallas kernels, per_device(): pl.pallas_call(kernel, out_shape=jax.ShapeDtypeStruct((64, 2048), BF), in...  187 us

profile of v4, /device:TPU:0, one launch (start us, length us, event | category | flops | bytes accessed | tf_op | source)
XLA Modules:
  0.0 189.1 jit_solution(10241434338102124510)
XLA Ops:
  0.0 187.4 %moe_decode.1 = bf16[64,2048]{1,0:T(8,128)(2,1)} custom-call(bf16[64,2048]{1,0:T(8,128)(2,1)} %bitcast.12, bf16[4,16,2048]{2,1,0:T(8,128)(2,1)} %q_ref.1, bf16[4,16,256]{2,1,0:T(8,128)(2,1)} %nk_ref.1, bf16[4,16,256]{2,1,0:T(8,128)(2,1)} %nv_ref.1, bf16[2048]{0:T(1024)(128)(2,1)} %gain_ref.1, s32[4,8,16]{2,1,0:T(8,128)} %bitcast.13, s32[16]{0:T(128)} %len_ref.1, ...), custom_call_target="tpu_custom_call" | custom-call | tf_op jit(solution)/shard_map/moe_decode/pallas_call | solution.py:600
  187.4 1.7 copy.16
